TPU v7x, 512 devices: a whole 4x4x16 slice. The times are simulated.
512 devices in a mesh: latent: 128 (over x, z, core), tok: 4 (over y).
Axes of the slice: x: 4, y: 4, z: 16, core: 2. Of those that a mesh axis runs over, the one named last changes fastest.
Arguments:
- tokens: bfloat16 [16384, 8192], P('latent', 'tok'), may hold values from -6 to 6
- blocks: int32 [16384, 2], P('latent'), may hold values from 0 to 127, all different within a row; in each aligned block of 128 rows (0 to 127, 128 to 255, ...) at most 3 rows name the same one
- slots: int32 [16384, 64], P('latent'), may hold values from 0 to 255, all different within a row
- enc_weight: bfloat16 [16384, 8192], P('latent', 'tok'), may hold values from -0.0625 to 0.0625
- dec_weight: bfloat16 [16384, 8192], P('latent', 'tok'), may hold values from -0.75 to 0.75
- enc_bias: float32 [16384], P('latent'), may hold values from -3 to 3
Outputs:
- grad_enc: bfloat16 [16384, 8192], P('latent', 'tok')
- grad_dec: bfloat16 [16384, 8192], P('latent', 'tok')
Inputs may be any that keep to these rules, and one draw needn't show every extreme that they name: Each row names 2 different blocks; the rows of one index of latent name one block at most 3 times. `slots`: each row names 64 different positions of the 2 blocks of its token; every position is named by some row.
All inputs are finite; a program needn't handle non-finite values.
Results may differ from a plain program's by a relative error of at most 0.0057.
Values may be sent and summed in bfloat16 or wider, within the bound.
A program may use at most 64 MiB of HBM per device.

v0:
```python
import math

import jax
import jax.numpy as jnp
from jax import lax
from jax.sharding import PartitionSpec as P


def contract(left, right, left_dim, right_dim):
    return lax.dot_general(
        left, right, (((left_dim,), (right_dim,)), ((), ())), preferred_element_type=jnp.float32
    )


def local(tokens, blocks, slots, enc_weight, dec_weight, enc_bias):
    tok_rows, feat_width = tokens.shape
    latents = enc_weight.shape[0]
    spread = blocks.shape[1]
    top_count = slots.shape[1]
    shards = lax.axis_size("latent")
    pair_total = tok_rows * spread
    capacity = pair_total // shards + max(1, pair_total // (8 * shards))
    slot_count = shards * capacity
    target = blocks.reshape(-1)
    onehot = (target[:, None] == jnp.arange(shards, dtype=jnp.int32)[None, :]).astype(jnp.int32)
    slot_rank = jnp.sum(onehot * jnp.cumsum(onehot, axis=0), axis=1) - 1
    slot_index = target * capacity + slot_rank
    row_index = jnp.arange(tok_rows, dtype=jnp.int32)[:, None]
    membership = jnp.zeros((tok_rows, spread, latents), jnp.bfloat16)
    membership = (
        membership.at[row_index, slots // latents, slots % latents]
        .set(1.0)
        .reshape(pair_total, latents)
    )
    doubled = jnp.repeat(tokens, spread, axis=0)
    send_rows = jnp.zeros((slot_count, feat_width), jnp.bfloat16).at[slot_index].set(doubled)
    send_mask = jnp.zeros((slot_count, latents), jnp.bfloat16).at[slot_index].set(membership)
    recv_rows, recv_mask = (
        lax.all_to_all(send_rows, "latent", split_axis=0, concat_axis=0, tiled=True),
        lax.all_to_all(send_mask, "latent", split_axis=0, concat_axis=0, tiled=True),
    )
    mask_wide = recv_mask.astype(jnp.float32)
    part_pre = contract(recv_rows, enc_weight, 1, 1)
    pre_acts = lax.psum(part_pre, "tok")
    code_values = (mask_wide * (pre_acts + enc_bias[None, :])).astype(jnp.bfloat16)
    partial_value = jnp.dot(code_values, dec_weight, preferred_element_type=jnp.float32).astype(
        jnp.bfloat16
    )
    returned = lax.all_to_all(partial_value, "latent", split_axis=0, concat_axis=0, tiled=True)
    picked = returned[slot_index].astype(jnp.float32).reshape(tok_rows, spread, feat_width)
    rebuilt = jnp.sum(picked, axis=1)
    error_rows = (rebuilt - tokens.astype(jnp.float32)).astype(jnp.bfloat16)
    send_errors = (
        jnp.zeros((slot_count, feat_width), jnp.bfloat16)
        .at[slot_index]
        .set(jnp.repeat(error_rows, spread, axis=0))
    )
    recv_errors = lax.all_to_all(send_errors, "latent", split_axis=0, concat_axis=0, tiled=True)
    part_back = contract(recv_errors, dec_weight, 1, 1)
    back_sum = lax.psum(part_back, "tok")
    back_grad = (mask_wide * back_sum).astype(jnp.bfloat16)
    grad_scale = math.sqrt(latents / (tok_rows * top_count))
    grad_dec = (contract(code_values, recv_errors, 0, 0) * grad_scale).astype(jnp.bfloat16)
    grad_enc = (contract(back_grad, recv_rows, 0, 0) * grad_scale).astype(jnp.bfloat16)
    return (grad_enc, grad_dec)


def solution(mesh):
    placed = (
        P("latent", "tok"),
        P("latent", None),
        P("latent", None),
        P("latent", "tok"),
        P("latent", "tok"),
        P("latent"),
    )
    return jax.shard_map(
        local,
        mesh=mesh,
        in_specs=placed,
        out_specs=(P("latent", "tok"), P("latent", "tok")),
        check_vma=False,
    )
```

profile of v0, /device:TPU:1, one launch (start us, length us, event | category | flops | bytes accessed | tf_op | source)
XLA Modules:
  0.0 526.2 jit_solution(7501791714838805519)
XLA Ops:
  7.2 0.0 copy-start
  7.2 0.0 copy-start.5
  7.2 0.9 copy.9
  8.1 0.1 eq.31
  8.2 0.1 eq.27
  8.3 0.7 broadcast_multiply_fusion
  9.0 0.1 copy.11
  9.1 0.2 fusion.6
  9.4 0.2 fusion.7
  9.6 0.1 copy.8
  9.7 0.1 mul.33
  9.9 0.0 copy-done.5
  9.9 0.6 broadcast_in_dim.39
  10.5 1.2 reshape.112
  11.8 3.3 scatter_custom_fusion.1
  15.1 2.3 all_to_all.32
  17.4 20.5 %all-to-all-start.1 = ((bf16[128,3,2048]{2,1,0:T(4,128)(2,1)}), bf16[128,3,2048]{2,1,0:T(4,128)(2,1)S(1)}, u32[]{:S(2)}, u32[]{:S(2)}) async-start(bf16[128,3,2048]{2,1,0:T(4,128)(2,1)} %all_to_all.32), calls=%async_computation.1 | async-start | bytes 4194304 | tf_op jit(solution)/shard_map/all_to_all | solution.py:39
  38.0 0.0 copy-done.7
  38.0 0.0 copy-done.10
  38.0 0.1 multiply_reduce_fusion
  38.1 0.0 copy-done.9
  38.1 0.1 and_reduce_fusion
  38.2 0.1 copy.13
  38.3 0.1 reshape.124
  38.4 56.6 %scatter_custom_fusion.3 = bf16[32768]{0:T(1024)(128)(2,1)S(1)} fusion(s32[8192]{0:T(1024)S(1)} %reshape.124, bf16[8192]{0:T(1024)(128)(2,1)S(1)} %broadcast.97, bf16[]{:T(256)} %constant.24.clone.1), kind=kCustom, calls=%fused_computation.40 | custom fusion | bytes 65538
  95.0 1.2 scatter_custom_fusion
  96.2 0.7 all_to_all.30
  96.9 40.2 %all-to-all-done.1 = bf16[128,3,2048]{2,1,0:T(4,128)(2,1)S(1)} async-done(((bf16[128,3,2048]{2,1,0:T(4,128)(2,1)}), bf16[128,3,2048]{2,1,0:T(4,128)(2,1)S(1)}, u32[]{:S(2)}, u32[]{:S(2)}) %all-to-all-start.1) | async-done | bytes 1572896 | tf_op jit(solution)/shard_map/all_to_all | solution.py:39
  137.1 8.7 %all-to-all-start = ((bf16[128,3,128]{2,1,0:T(4,128)(2,1)}), bf16[128,3,128]{2,1,0:T(4,128)(2,1)S(1)}, u32[]{:S(2)}, u32[]{:S(2)}) async-start(bf16[128,3,128]{2,1,0:T(4,128)(2,1)} %all_to_all.30), calls=%async_computation | async-start | bytes 262144 | tf_op jit(solution)/shard_map/all_to_all | solution.py:40
  145.8 0.0 copy-done.4
  145.8 0.0 all-reduce.3.cloned.1.call-start
  145.9 0.0 copy-start.6
  145.9 4.0 all_to_all.34
  149.9 0.0 copy-start.8
  149.9 1.3 fusion.19
  151.2 0.0 all-reduce.3.cloned.1.call-update
  151.2 12.0 %all-to-all-done = bf16[128,3,128]{2,1,0:T(4,128)(2,1)S(1)} async-done(((bf16[128,3,128]{2,1,0:T(4,128)(2,1)}), bf16[128,3,128]{2,1,0:T(4,128)(2,1)S(1)}, u32[]{:S(2)}, u32[]{:S(2)}) %all-to-all-start) | async-done | bytes 98336 | tf_op jit(solution)/shard_map/all_to_all | solution.py:40
  163.2 0.1 reshape.90
  163.3 43.9 %all-reduce.3.cloned.1.call-done = f32[384,128]{1,0:T(8,128)} async-done(((f32[384,128]{1,0:T(8,128)}), f32[384,128]{1,0:T(8,128)}) %all-reduce.3.cloned.1.call-update) | async-done | bytes 196624 | tf_op jit(solution)/shard_map/psum | solution.py:44
  207.3 1.0 multiply_convert_fusion.1
  208.2 0.0 copy-done.1
  208.2 0.0 copy-done
  208.2 1.7 convolution_convert_fusion
  209.9 5.1 all_to_all.35
  215.1 19.2 %all-to-all-start.2 = ((bf16[128,3,2048]{2,1,0:T(4,128)(2,1)}), bf16[128,3,2048]{2,1,0:T(4,128)(2,1)}, u32[]{:S(2)}, u32[]{:S(2)}) async-start(bf16[128,3,2048]{2,1,0:T(4,128)(2,1)} %all_to_all.35), calls=%async_computation.2 | async-start | bytes 4194304 | tf_op jit(solution)/shard_map/all_to_all | solution.py:49
  234.3 0.0 all-reduce.5.cloned.1.call-start
  234.3 98.7 %all-to-all-done.2 = bf16[128,3,2048]{2,1,0:T(4,128)(2,1)} async-done(((bf16[128,3,2048]{2,1,0:T(4,128)(2,1)}), bf16[128,3,2048]{2,1,0:T(4,128)(2,1)}, u32[]{:S(2)}, u32[]{:S(2)}) %all-to-all-start.2) | async-done | bytes 1572896 | tf_op jit(solution)/shard_map/all_to_all | solution.py:49
  333.0 3.9 all_to_all.37
  337.0 2.3 gather_fusion
  339.3 2.4 reshape.91
  341.7 3.9 reduce_sum.19
  345.6 1.3 subtract_convert_fusion
  346.9 0.6 broadcast_in_dim.40
  347.6 0.4 reshape.120
  348.0 3.4 scatter_custom_fusion.2
  351.5 4.0 all_to_all.38
  355.5 107.8 %all_to_all.45 = bf16[128,3,2048]{2,1,0:T(4,128)(2,1)} all-to-all(bf16[128,3,2048]{2,1,0:T(4,128)(2,1)S(1)} %all_to_all.38), channel_id=1, replica_groups=mesh['latent'=128,'tok'=4] {'latent'}, dimensions={0} | all-to-all | bytes 3145728 | tf_op jit(solution)/shard_map/all_to_all | solution.py:58
  463.2 3.9 all_to_all.40
  467.2 1.1 copy-done.3
  468.3 1.2 fusion.20
  469.5 0.0 all-reduce.5.cloned.1.call-update
  469.6 2.8 fusion.1
  472.4 44.8 %all-reduce.5.cloned.1.call-done = f32[384,128]{1,0:T(8,128)} async-done(((f32[384,128]{1,0:T(8,128)}), f32[384,128]{1,0:T(8,128)}) %all-reduce.5.cloned.1.call-update) | async-done | bytes 196624 | tf_op jit(solution)/shard_map/psum | solution.py:60
  517.1 2.2 fusion
  (23 shorter events, 0.2 us)
Async XLA Ops:
  7.2 201.1 %copy-start = (bf16[128,2048]{1,0:T(8,128)(2,1)S(1)}, bf16[128,2048]{1,0:T(8,128)(2,1)}, u32[]{:S(2)}) copy-start(bf16[128,2048]{1,0:T(8,128)(2,1)} %param.10) | copy-start | bytes 1572868
  7.2 2.7 copy-start.5
  17.4 20.5 %copy-start.7 = (s32[128,64]{0,1:T(8,128)S(1)}, s32[128,64]{0,1:T(8,128)}, u32[]{:S(2)}) copy-start(s32[128,64]{0,1:T(8,128)} %param.8) | copy-start | bytes 98308
  17.4 20.6 %copy-start.10 = (s32[3]{0:T(128)S(1)}, s32[3]{0:T(128)}, u32[]{:S(2)}) copy-start(s32[3]{0:T(128)} %constant.57) | copy-start | bytes 40
  17.4 20.7 %copy-start.9 = (s32[3]{0:T(128)S(1)}, s32[3]{0:T(128)}, u32[]{:S(2)}) copy-start(s32[3]{0:T(128)} %constant.60) | copy-start | bytes 40
  17.4 119.7 %all-to-all-start.1 = ((bf16[128,3,2048]{2,1,0:T(4,128)(2,1)}), bf16[128,3,2048]{2,1,0:T(4,128)(2,1)S(1)}, u32[]{:S(2)}, u32[]{:S(2)}) async-start(bf16[128,3,2048]{2,1,0:T(4,128)(2,1)} %all_to_all.32), calls=%async_computation.1 | async-start | bytes 4194304 | tf_op jit(solution)/shard_map/all_to_all | solution.py:39
  137.1 8.7 %copy-start.4 = (bf16[128,3,2048]{2,1,0:T(4,128)(2,1)}, bf16[128,3,2048]{2,1,0:T(4,128)(2,1)S(1)}, u32[]{:S(2)}) copy-start(bf16[128,3,2048]{2,1,0:T(4,128)(2,1)S(1)} %all-to-all-done.1) | copy-start | bytes 4718596
  137.1 26.1 %all-to-all-start = ((bf16[128,3,128]{2,1,0:T(4,128)(2,1)}), bf16[128,3,128]{2,1,0:T(4,128)(2,1)S(1)}, u32[]{:S(2)}, u32[]{:S(2)}) async-start(bf16[128,3,128]{2,1,0:T(4,128)(2,1)} %all_to_all.30), calls=%async_computation | async-start | bytes 262144 | tf_op jit(solution)/shard_map/all_to_all | solution.py:40
  145.8 61.4 %all-reduce.3.cloned.1.call-start = ((), (), s32[]{:S(2)}) async-start(), calls=%async_computation.4 | async-start | bytes 393216 | tf_op jit(solution)/shard_map/psum | solution.py:44
  145.9 4.0 copy-start.6
  149.9 58.3 %copy-start.1 = (bf16[384,2048]{1,0:T(8,128)(2,1)}, bf16[384,2048]{1,0:T(8,128)(2,1)S(1)}, u32[]{:S(2)}) copy-start(bf16[384,2048]{1,0:T(8,128)(2,1)S(1)} %all_to_all.34) | copy-start | bytes 4718596
  149.9 57.3 %copy-start.8 = (f32[128]{0:T(128)S(1)}, f32[128]{0:T(128)}, u32[]{:S(2)}) copy-start(f32[128]{0:T(128)} %param.11) | copy-start | bytes 1540
  215.1 118.0 %all-to-all-start.2 = ((bf16[128,3,2048]{2,1,0:T(4,128)(2,1)}), bf16[128,3,2048]{2,1,0:T(4,128)(2,1)}, u32[]{:S(2)}, u32[]{:S(2)}) async-start(bf16[128,3,2048]{2,1,0:T(4,128)(2,1)} %all_to_all.35), calls=%async_computation.2 | async-start | bytes 4194304 | tf_op jit(solution)/shard_map/all_to_all | solution.py:49
  234.3 282.9 %all-reduce.5.cloned.1.call-start = ((), (), s32[]{:S(2)}) async-start(), calls=%async_computation.5 | async-start | bytes 393216 | tf_op jit(solution)/shard_map/psum | solution.py:60
  467.1 1.2 copy-start.3
  469.5 47.6 %copy-start.2 = (bf16[384,2048]{1,0:T(8,128)(2,1)S(1)}, bf16[384,2048]{1,0:T(8,128)(2,1)}, u32[]{:S(2)}) copy-start(bf16[384,2048]{1,0:T(8,128)(2,1)} %copy-done.1) | copy-start | bytes 4718596
Sparse Core Ops, SparseCore 0:
  151.3 55.8 all-reduce.2
  469.7 47.4 all-reduce.4
where the time goes:
time: 528 us; the launch traced here: 526 us
  waiting for transfers between devices  240 us (45%)
  blocking collectives  108 us (20%)
  local copies, waits for them, and re-layouts  99.1 us (19%)
  starting transfers between devices  48.5 us (9%)
  between operations  14.4 us (3%)
  matrix products  9.2 us (2%)
  other arithmetic  7.54 us (1%)
    all_to_all x1, blocking collectives, local(): lax.all_to_all(send_errors, 'latent', split_axis=0, concat_axis=0, tiled=...  108 us
    all_to_all x1, waiting for transfers between devices, local(): lax.all_to_all(partial_value, 'latent', split_axis=0, concat_axis=0, tile...  98.7 us
    unnamed x28, local copies, waits for them, and re-layouts  58.8 us
    psum x1, waiting for transfers between devices, local(): back_sum = lax.psum(part_back, 'tok')  44.8 us
    psum x1, waiting for transfers between devices, local(): pre_acts = lax.psum(part_pre, 'tok')  43.9 us
    all_to_all x1, waiting for transfers between devices, local(): lax.all_to_all(send_rows, 'latent', split_axis=0, concat_axis=0, tiled=True)  40.2 us
    all_to_all x1, starting transfers between devices, local(): lax.all_to_all(send_rows, 'latent', split_axis=0, concat_axis=0, tiled=True)  20.5 us
    all_to_all x1, starting transfers between devices, local(): lax.all_to_all(partial_value, 'latent', split_axis=0, concat_axis=0, tile...  19.2 us
  transfers between devices with their start and end apart: 5, of which 5 were waited for; matrix products, arithmetic and copies ran while one was open for 12% of the time, Pallas kernels for 0%

commit v1 on v0

v1 whole, which is shorter than its diff:
```python
import functools
import math

import jax
import jax.numpy as jnp
from jax import lax
from jax.experimental import pallas as pl
from jax.experimental.pallas import tpu as pltpu
from jax.sharding import PartitionSpec as P

MESH = pl.DeviceIdType.MESH
F32 = jnp.float32
BF16 = jnp.bfloat16

NX, NZ, NC = 4, 16, 2
N = NX * NZ * NC
HALF = N // NC
CAP = 3
NY = 4
SUB = 16
LANE = 128
CHUNK = CAP * NZ


def latent_index(x, z, c):
    return (x * NZ + z) * NC + c


def inner_index(x, z, c):
    return (c * NX + x) * NZ + z


def z_step(k):
    return jnp.where(lax.rem(k, 2) == 1, (k + 1) // 2, NZ - k // 2)


def kernel(
    tokens, blocks, slots, enc, dec, bias,
    genc, gdec,
    sx, rx, sp, rp, se, re, sm, rm,
    nat, xnat, enat, st, smat, mem,
    part_f, part_b, sum_f, sum_b, codes, back, mask,
    sx_sem, sp_sem, se_sem, sm_sem, rx_sem, rp_sem, re_sem, rm_sem,
    sf_sem, rf_sem, sg_sem, rg_sem,
):
    width = tokens.shape[1]
    rows = tokens.shape[0]
    me = lax.axis_index("latent")
    y = lax.axis_index("tok")
    c = lax.rem(me, NC)
    z = lax.rem(me // NC, NZ)
    x = me // (NC * NZ)
    mine = inner_index(x, z, c)

    def partner(k):
        dz, rest = k // (NX * NC), lax.rem(k, NX * NC)
        px = lax.rem(x + rest // NC, NX)
        pz = lax.rem(z + z_step(dz), NZ)
        pc = lax.rem(c + lax.rem(rest, NC), NC)
        return px, pz, pc

    barrier = pltpu.get_barrier_semaphore()

    def greet(k, _):
        pl.semaphore_signal(
            barrier, inc=1, device_id={"latent": latent_index(*partner(k))}, device_id_type=MESH
        )
        return 0

    lax.fori_loop(1, N, greet, 0)
    for k in range(1, NY):
        pl.semaphore_signal(
            barrier, inc=1, device_id={"tok": lax.rem(y + k, NY)}, device_id_type=MESH
        )

    row = lax.broadcasted_iota(jnp.int32, (256, 256), 0)
    col = lax.broadcasted_iota(jnp.int32, (256, 256), 1)
    swap = jnp.where(
        (row // SUB == lax.rem(col, SUB)) & (lax.rem(row, SUB) == col // SUB), 1.0, 0.0
    ).astype(BF16)

    def to_tiles(src, row0, dst, place, rank):
        block = src[pl.ds(row0, SUB), :]
        stacked = jnp.concatenate(
            [block[:, i * LANE : (i + 1) * LANE] for i in range(width // LANE)], axis=0
        )
        out = jnp.dot(swap, stacked, preferred_element_type=F32).astype(BF16)
        dst[pl.ds(place, SUB), rank] = out.reshape(SUB, SUB, LANE)

    def to_rows(src, place, rank, dst, row0):
        block = src[pl.ds(place, SUB), rank].reshape(SUB * SUB, LANE)
        out = jnp.dot(swap, block, preferred_element_type=F32).astype(BF16)
        dst[pl.ds(row0, SUB), :] = jnp.concatenate(
            [out[i * SUB : (i + 1) * SUB, :] for i in range(width // LANE)], axis=1
        )

    lanes = lax.broadcasted_iota(jnp.int32, (rows, N), 1)
    subs = lax.broadcasted_iota(jnp.int32, (rows, N), 0)
    named = blocks[...]
    place = lax.rem(named, NC) * HALF + named // NC
    hot = [jnp.where(place[:, b : b + 1] == lanes, 1.0, 0.0) for b in range(2)]
    lower = jnp.where(lanes < subs, 1.0, 0.0).astype(BF16)
    ahead0 = jnp.dot(lower, hot[0].astype(BF16), preferred_element_type=F32)
    ahead1 = jnp.dot(lower, hot[1].astype(BF16), preferred_element_type=F32) + jnp.sum(
        hot[0], axis=0, keepdims=True
    )
    for r in range(CAP):
        s0 = hot[0] * jnp.where(ahead0 == r, 1.0, 0.0)
        s1 = hot[1] * jnp.where(ahead1 == r, 1.0, 0.0)
        st[:, r * N : (r + 1) * N] = (s0 + s1).astype(BF16)
        smat[0, r * N : (r + 1) * N, :] = s0.T.astype(BF16)
        smat[1, r * N : (r + 1) * N, :] = s1.T.astype(BF16)

    step = 512

    def spread(src):
        def one(i, _):
            cols = pl.ds(pl.multiple_of(i * step, step), step)
            both = smat[0] + smat[1]
            nat[:, cols] = jnp.dot(both, src[:, cols], preferred_element_type=F32).astype(BF16)
            return 0

        lax.fori_loop(0, width // step, one, 0)

    def pack(dst):
        def one(g, _):
            r, d = g // (N // SUB), lax.rem(g, N // SUB)
            to_tiles(nat, pl.multiple_of(g * SUB, SUB), dst, d * SUB, r)
            return 0

        lax.fori_loop(0, CAP * N // SUB, one, 0)

    def send_rows(src, dst, send_sem, recv_sem):
        pltpu.make_async_copy(src.at[mine], dst.at[mine], recv_sem.at[c]).start()

        def one(k, _):
            px, pz, pc = partner(k)
            pltpu.make_async_remote_copy(
                src_ref=src.at[inner_index(px, pz, pc)],
                dst_ref=dst.at[mine],
                send_sem=send_sem,
                recv_sem=recv_sem.at[c],
                device_id={"latent": latent_index(px, pz, pc)},
                device_id_type=MESH,
            ).start()
            return 0

        lax.fori_loop(1, N, one, 0)

    def take(ref, sem):
        pltpu.make_async_copy(ref, ref, sem).wait()

    spread(tokens)
    pack(sx)
    pl.semaphore_wait(barrier, N - 1 + NY - 1)

    @pl.when(c == 0)
    def _():
        send_rows(sx, rx, sx_sem, rx_sem)

    ids = slots[...]
    member = [jnp.zeros((rows, LANE), F32) for _ in range(2)]
    for k in range(slots.shape[1]):
        one_id = ids[:, k : k + 1]
        member = [jnp.where(one_id == lanes + b * LANE, 1.0, member[b]) for b in range(2)]
    for b in range(2):
        mem[b] = member[b].astype(BF16)
    slot_mask = (
        jnp.dot(smat[0], mem[0], preferred_element_type=F32)
        + jnp.dot(smat[1], mem[1], preferred_element_type=F32)
    ).astype(BF16)
    ri = lax.broadcasted_iota(jnp.int32, (SUB * SUB, CHUNK), 0)
    ci = lax.broadcasted_iota(jnp.int32, (SUB * SUB, CHUNK), 1)
    pick = jnp.where(
        (lax.rem(ri, SUB) == ci // SUB) & (ri // SUB == lax.rem(ci, SUB)), 1.0, 0.0
    ).astype(BF16)
    for g in range(N // SUB):
        three = jnp.concatenate(
            [slot_mask[r * N + g * SUB : r * N + (g + 1) * SUB, :] for r in range(CAP)], axis=0
        )
        out = jnp.dot(pick, three, preferred_element_type=F32).astype(BF16)
        sm[g * SUB : (g + 1) * SUB] = out.reshape(SUB, SUB, LANE)

    def send_mask():
        spot = c * NZ + z
        pltpu.make_async_copy(sm.at[mine], rm.at[spot], rm_sem.at[c]).start()

        def one(k, _):
            px, pz, pc = partner(k)
            pltpu.make_async_remote_copy(
                src_ref=sm.at[inner_index(px, pz, pc)],
                dst_ref=rm.at[spot],
                send_sem=sm_sem,
                recv_sem=rm_sem.at[c],
                device_id={"latent": latent_index(px, pz, pc)},
                device_id_type=MESH,
            ).start()
            return 0

        lax.fori_loop(1, N, one, 0)

    @pl.when((x == y) & (c == 0))
    def _():
        send_mask()

    def unpack(src, dst, h):
        def one(i, _):
            g = h * (HALF // SUB * CAP) + i
            to_rows(src, (g // CAP) * SUB, lax.rem(g, CAP), dst, pl.multiple_of(g * SUB, SUB))
            return 0

        lax.fori_loop(0, HALF // SUB * CAP, one, 0)

    def contract(left, right, h):
        lhs = left[pl.ds(h * NX * CHUNK, NX * CHUNK), :]
        out = lax.dot_general(lhs, right[...], (((1,), (1,)), ((), ())), preferred_element_type=F32)
        return out.reshape(NX, CHUNK, LANE)

    def scatter(part, total, h, q):
        for k in range(1, NY):
            p = lax.rem(y + k, NY)
            pltpu.make_async_remote_copy(
                src_ref=part.at[h, p],
                dst_ref=total.at[h, k],
                send_sem=sf_sem.at[q, h],
                recv_sem=rf_sem.at[q, h],
                device_id={"tok": p},
                device_id_type=MESH,
            ).start()

    def summed(part, total, h, q):
        take(total.at[h, pl.ds(1, NY - 1)], rf_sem.at[q, h])
        out = part[h, y]
        for k in range(1, NY):
            out = out + total[h, k]
        return out

    def gather(values, h, q):
        for k in range(1, NY):
            pltpu.make_async_remote_copy(
                src_ref=values.at[h, y],
                dst_ref=values.at[h, y],
                send_sem=sg_sem.at[q, h],
                recv_sem=rg_sem.at[q, h],
                device_id={"tok": lax.rem(y + k, NY)},
                device_id_type=MESH,
            ).start()

    def gathered(values, h, q):
        take(values.at[h, pl.ds(0, NY - 1)], rg_sem.at[q, h])

    def forward(h):
        unpack(rx, xnat, h)
        part_f[h] = contract(xnat, enc, h)
        scatter(part_f, sum_f, h, 0)
        take(rm.at[pl.ds(h * NZ, NZ)], rm_sem.at[h])
        got = rm[h * NZ : (h + 1) * NZ].reshape(NZ * SUB, LANE)
        mask[h] = lax.dot_general(pick, got, (((0,), (0,)), ((), ())), preferred_element_type=F32)
        total = summed(part_f, sum_f, h, 0)
        codes[h, y] = (mask[h] * (total + bias[...])).astype(BF16)
        gather(codes, h, 0)
        gathered(codes, h, 0)
        mine_codes = codes[h].reshape(NX * CHUNK, LANE)

        def product(i, _):
            cols = pl.ds(pl.multiple_of(i * step, step), step)
            nat[pl.ds(h * NX * CHUNK, NX * CHUNK), cols] = jnp.dot(
                mine_codes, dec[:, cols], preferred_element_type=F32
            ).astype(BF16)
            return 0

        lax.fori_loop(0, width // step, product, 0)

        def one(i, _):
            g = h * (HALF // SUB * CAP) + i
            to_tiles(nat, pl.multiple_of(g * SUB, SUB), sp, (g // CAP) * SUB, lax.rem(g, CAP))
            return 0

        lax.fori_loop(0, HALF // SUB * CAP, one, 0)

        def send(k, _):
            px, pz = lax.rem(x + lax.rem(k, NX), NX), lax.rem(z + z_step(k // NX), NZ)
            pltpu.make_async_remote_copy(
                src_ref=sp.at[inner_index(px, pz, h)],
                dst_ref=rp.at[mine],
                send_sem=sp_sem.at[h],
                recv_sem=rp_sem,
                device_id={"latent": latent_index(px, pz, h)},
                device_id_type=MESH,
            ).start()
            return 0

        @pl.when(c == h)
        def _():
            pltpu.make_async_copy(sp.at[mine], rp.at[mine], rp_sem).start()

        @pl.when(c != h)
        def _():
            send(0, 0)

        lax.fori_loop(1, HALF, send, 0)

    take(rx.at[pl.ds(0, HALF)], rx_sem.at[0])

    @pl.when(c == 1)
    def _():
        send_rows(sx, rx, sx_sem, rx_sem)

    @pl.when((x == y) & (c == 1))
    def _():
        send_mask()

    forward(0)
    take(rx.at[pl.ds(HALF, HALF)], rx_sem.at[1])
    forward(1)

    take(rp, rp_sem)

    def returned(g, _):
        r, d = g // (N // SUB), lax.rem(g, N // SUB)
        to_rows(rp, d * SUB, r, nat, pl.multiple_of(g * SUB, SUB))
        return 0

    lax.fori_loop(0, CAP * N // SUB, returned, 0)

    def error(i, _):
        cols = pl.ds(pl.multiple_of(i * step, step), step)
        recon = jnp.dot(st[...], nat[:, cols], preferred_element_type=F32)
        err = (recon - tokens[:, cols].astype(F32)).astype(BF16)
        nat[:, cols] = jnp.dot(
            smat[0] + smat[1], err, preferred_element_type=F32
        ).astype(BF16)
        return 0

    lax.fori_loop(0, width // step, error, 0)
    pack(se)
    send_rows(se, re, se_sem, re_sem)

    def backward(h):
        take(re.at[pl.ds(h * HALF, HALF)], re_sem.at[h])
        unpack(re, enat, h)
        part_b[h] = contract(enat, dec, h)
        scatter(part_b, sum_b, h, 1)
        total = summed(part_b, sum_b, h, 1)
        back[h, y] = (mask[h] * total).astype(BF16)
        gather(back, h, 1)

    backward(0)
    backward(1)
    scale = math.sqrt(LANE / (rows * slots.shape[1]))

    def gradient(values, other, out):
        left = values[...].reshape(CAP * N, LANE).astype(F32).T.astype(BF16)

        def one(i, _):
            cols = pl.ds(pl.multiple_of(i * step, step), step)
            out[:, cols] = (
                jnp.dot(left, other[:, cols], preferred_element_type=F32) * scale
            ).astype(BF16)
            return 0

        lax.fori_loop(0, width // step, one, 0)

    gradient(codes, enat, gdec)
    gathered(back, 0, 1)
    gathered(back, 1, 1)
    gradient(back, xnat, genc)

    take(sx.at[pl.ds(0, N - 1)], sx_sem)
    take(se.at[pl.ds(0, N - 1)], se_sem)

    @pl.when(x == y)
    def _():
        take(sm.at[pl.ds(0, N - 1)], sm_sem)

    for h in range(NC):

        @pl.when(c == h)
        def _(h=h):
            take(sp.at[pl.ds(0, HALF - 1)], sp_sem.at[h])

        @pl.when(c != h)
        def _(h=h):
            take(sp.at[pl.ds(0, HALF)], sp_sem.at[h])

        take(part_f.at[h, pl.ds(0, NY - 1)], sf_sem.at[0, h])
        take(part_b.at[h, pl.ds(0, NY - 1)], sf_sem.at[1, h])
        take(codes.at[h, pl.ds(0, NY - 1)], sg_sem.at[0, h])
        take(back.at[h, pl.ds(0, NY - 1)], sg_sem.at[1, h])


def local(tokens, blocks, slots, enc, dec, bias):
    rows, width = tokens.shape
    tiles = pltpu.VMEM((N, CAP, SUB, LANE), BF16)
    dense = pltpu.VMEM((CAP * N, width), BF16)
    shares = pltpu.VMEM((NC, NY, CHUNK, LANE), F32)
    shares16 = pltpu.VMEM((NC, NY, CHUNK, LANE), BF16)
    dma = pltpu.SemaphoreType.DMA
    return pl.pallas_call(
        kernel,
        out_shape=[jax.ShapeDtypeStruct((rows, width), BF16)] * 2,
        in_specs=[pl.BlockSpec(memory_space=pltpu.VMEM)] * 6,
        out_specs=[pl.BlockSpec(memory_space=pltpu.VMEM)] * 2,
        scratch_shapes=[tiles] * 6
        + [
            pltpu.VMEM((N, SUB, LANE), BF16),
            pltpu.VMEM((NC * NZ, SUB, LANE), BF16),
            dense,
            dense,
            dense,
            pltpu.VMEM((rows, CAP * N), BF16),
            pltpu.VMEM((2, CAP * N, rows), BF16),
            pltpu.VMEM((2, rows, LANE), BF16),
            shares,
            shares,
            shares,
            shares,
            shares16,
            shares16,
            pltpu.VMEM((NC, CHUNK, LANE), F32),
            dma,
            dma((NC,)),
            dma,
            dma,
            dma((NC,)),
            dma,
            dma((NC,)),
            dma((NC,)),
            dma((2, NC)),
            dma((2, NC)),
            dma((2, NC)),
            dma((2, NC)),
        ],
        compiler_params=pltpu.CompilerParams(
            collective_id=0, has_side_effects=True, vmem_limit_bytes=40 << 20
        ),
    )(tokens, blocks, slots, enc, dec, bias.reshape(1, -1))


def solution(mesh):
    placed = (
        P("latent", "tok"),
        P("latent", None),
        P("latent", None),
        P("latent", "tok"),
        P("latent", "tok"),
        P("latent"),
    )
    return jax.shard_map(
        local,
        mesh=mesh,
        in_specs=placed,
        out_specs=(P("latent", "tok"), P("latent", "tok")),
        check_vma=False,
    )
```

time: 528 us -> 273 us (0.52)
  Pallas kernels: 0 us -> 264 us
  waiting for transfers between devices: 240 us -> 0 us
  blocking collectives: 108 us -> 0 us
  local copies, waits for them, and re-layouts: 99.1 us -> 6.79 us
  starting transfers between devices: 48.5 us -> 0 us
  between operations: 14.4 us -> 0.66 us
  matrix products: 9.2 us -> 0 us
  other arithmetic: 7.54 us -> 0 us
    pallas_call x0 -> x1, Pallas kernels: none -> 264 us  [local(): pl.pallas_call(kernel, out_shape=[jax.ShapeDtypeStruct((rows, width), BF1...]
    all_to_all x3 -> x0, waiting for transfers between devices: 151 us -> none  [the longest x1 98.7 us: local(): lax.all_to_all(partial_value, 'latent', split_axis=0, concat_axis=0, tile...]
    all_to_all x1 -> x0, blocking collectives: 108 us -> none  [local(): lax.all_to_all(send_errors, 'latent', split_axis=0, concat_axis=0, tiled=...]
    psum x2 -> x0, waiting for transfers between devices: 88.7 us -> none  [the longest x1 44.8 us: local(): back_sum = lax.psum(part_back, 'tok')]
    unnamed x28 -> x16, local copies, waits for them, and re-layouts: 58.8 us -> 6.79 us
    all_to_all x3 -> x0, starting transfers between devices: 48.4 us -> none  [the longest x1 20.5 us: local(): lax.all_to_all(send_rows, 'latent', split_axis=0, concat_axis=0, tiled=True)]
    all_to_all x7 -> x0, local copies, waits for them, and re-layouts: 24 us -> none  [the longest x2 9.06 us: local(): lax.all_to_all(partial_value, 'latent', split_axis=0, concat_axis=0, tile...]
    dot_general x5 -> x0, matrix products: 9.2 us -> none  [the longest x4 7.49 us: contract(): lax.dot_general(left, right, (((left_dim,), (right_dim,)), ((), ())), pre...]
  transfers between devices with their start and end apart: 5 -> 0, of which waited for: 5 -> 0; matrix products, arithmetic and copies ran while one was open for 12% -> 0% of each run, Pallas kernels for 0% -> 0%
where the time goes in v1:
time: 273 us; the launch traced here: 271 us
  Pallas kernels  264 us (97%)
  local copies, waits for them, and re-layouts  6.79 us (2%)
    pallas_call x1, Pallas kernels, local(): pl.pallas_call(kernel, out_shape=[jax.ShapeDtypeStruct((rows, width), BF1...  264 us
    unnamed x16, local copies, waits for them, and re-layouts  6.79 us

profile of v1, /device:TPU:1, one launch (start us, length us, event | category | flops | bytes accessed | tf_op | source)
XLA Modules:
  0.0 271.4 jit_solution(16085229063079854006)
XLA Ops:
  0.6 0.0 copy-start.5
  0.6 0.7 copy-done.5
  1.3 0.0 copy-start.4
  1.3 0.1 copy.8.blocks
  1.4 0.6 copy-done.4
  2.1 0.0 copy-start.3
  2.1 0.1 copy.9.slots
  2.2 0.6 copy-done.3
  2.7 0.0 copy-start
  2.7 1.0 copy-done
  3.8 0.0 copy-start.1
  3.8 1.0 copy-done.1
  4.8 0.0 copy-start.2
  4.8 1.0 copy-done.2
  5.9 264.0 %shard_map.77 = (bf16[128,2048]{1,0:T(8,128)(2,1)S(1)}, bf16[128,2048]{1,0:T(8,128)(2,1)S(1)}) custom-call(bf16[128,2048]{1,0:T(8,128)(2,1)S(1)} %copy-done, s32[128,2]{1,0:T(8,128)S(1)} %copy.8.blocks, s32[128,64]{1,0:T(8,128)S(1)} %copy.9.slots, bf16[128,2048]{1,0:T(8,128)(2,1)S(1)} %copy-done.1, bf16[128,2048]{1,0:T(8,128)(2,1)S(1)} %copy-done.2, ...), custom_call_target="tpu_custom_call" | custom-call | tf_op jit(solution)/shard_map/pallas_call | solution.py:399
  269.8 0.8 copy.12
  270.6 0.8 copy.13
Async XLA Ops:
  0.6 0.7 copy-start.5
  1.3 0.8 copy-start.4
  2.1 0.7 copy-start.3
  2.7 1.0 copy-start
  3.8 1.0 copy-start.1
  4.8 1.0 copy-start.2

commit v2 on v1

v2 whole, which is shorter than its diff:
```python
import functools
import math

import jax
import jax.numpy as jnp
from jax import lax
from jax.experimental import pallas as pl
from jax.experimental.pallas import tpu as pltpu
from jax.sharding import PartitionSpec as P

MESH = pl.DeviceIdType.MESH
F32 = jnp.float32
BF16 = jnp.bfloat16

NX, NZ, NC = 4, 16, 2
N = NX * NZ * NC
HALF = N // NC
CAP = 3
NY = 4
SUB = 16
LANE = 128
CHUNK = CAP * NZ
SPLIT = N // 2
FIRST = 32


def latent_index(x, z, c):
    return (x * NZ + z) * NC + c


def inner_index(x, z, c):
    return c * HALF + lax.rem(z, NY) * SUB + z // NY * NX + x


def z_step(k):
    return jnp.where(lax.rem(k, 2) == 1, (k + 1) // 2, NZ - k // 2)


def kernel(
    tokens_hbm, blocks, slots, enc_hbm, dec_hbm, bias,
    genc, gdec,
    tokens, enc, dec,
    sx, rx, sp, rp, se, re, s1, r1, s2, r2,
    nat, xnat, enat, smat, early,
    part_f, part_b, sum_f, sum_b, codes, back, mask,
    sx_sem, sp_sem, se_sem, s1_sem, s2_sem, rx_sem, rp_sem, re_sem, r1_sem, r2_sem,
    sf_sem, rf_sem, sg_sem, rg_sem, in_sem,
):
    width = tokens.shape[1]
    rows = tokens.shape[0]
    me = lax.axis_index("latent")
    y = lax.axis_index("tok")
    c = lax.rem(me, NC)
    z = lax.rem(me // NC, NZ)
    x = me // (NC * NZ)
    mine = inner_index(x, z, c)

    def partner(k):
        dz, rest = k // (NX * NC), lax.rem(k, NX * NC)
        px = lax.rem(x + rest // NC, NX)
        pz = lax.rem(z + z_step(dz), NZ)
        pc = lax.rem(c + lax.rem(rest, NC), NC)
        return px, pz, pc

    loads = [
        pltpu.make_async_copy(src, dst, in_sem.at[i])
        for i, (src, dst) in enumerate(((tokens_hbm, tokens), (enc_hbm, enc), (dec_hbm, dec)))
    ]
    loads[0].start()

    barrier = pltpu.get_barrier_semaphore()

    def greet(k, _):
        pl.semaphore_signal(
            barrier, inc=1, device_id={"latent": latent_index(*partner(k))}, device_id_type=MESH
        )
        return 0

    lax.fori_loop(1, N, greet, 0)
    for k in range(1, NY):
        pl.semaphore_signal(
            barrier, inc=1, device_id={"tok": lax.rem(y + k, NY)}, device_id_type=MESH
        )

    parts = width // LANE

    def to_tiles(src, row0, dst, place, rank):
        dst[place : place + SUB, rank] = pltpu.einshape(
            "a(bc)->abc", src[row0 : row0 + SUB, :], b=parts, c=LANE
        )

    def to_rows(src, place, rank, dst, row0):
        dst[row0 : row0 + SUB, :] = pltpu.einshape("abc->a(bc)", src[place : place + SUB, rank])

    lanes = lax.broadcasted_iota(jnp.int32, (N, rows), 1)
    subs = lax.broadcasted_iota(jnp.int32, (N, rows), 0)
    named = blocks[...]
    column = named // NC
    place = inner_index(column // NZ, lax.rem(column, NZ), lax.rem(named, NC))
    hot = [jnp.where(place[b : b + 1, :] == subs, 1.0, 0.0) for b in range(2)]
    upper = jnp.where(subs < lanes, 1.0, 0.0).astype(BF16)
    ahead0 = jnp.dot(hot[0].astype(BF16), upper, preferred_element_type=F32)
    ahead1 = jnp.dot(hot[1].astype(BF16), upper, preferred_element_type=F32) + jnp.sum(
        hot[0], axis=1, keepdims=True
    )
    rank = [
        jnp.sum(hot[b] * ahead, axis=0, keepdims=True) for b, ahead in enumerate((ahead0, ahead1))
    ]
    for r in range(CAP):
        smat[r * N : (r + 1) * N, :] = sum(
            hot[b] * jnp.where(rank[b] == r, 1.0, 0.0) for b in range(2)
        ).astype(BF16)

    step = 512

    def spread(src):
        def one(i, _):
            cols = pl.ds(pl.multiple_of(i * step, step), step)
            nat[:, cols] = jnp.dot(smat[...], src[:, cols], preferred_element_type=F32).astype(BF16)
            return 0

        lax.fori_loop(0, width // step, one, 0)

    def pack(dst):
        for g in range(CAP * N // SUB):
            to_tiles(nat, g * SUB, dst, g % (N // SUB) * SUB, g // (N // SUB))

    def send_rows(src, dst, send_sem, recv_sem, first=0, last=N - 1):
        def one(i, _):
            k = N - 1 - i
            px, pz, pc = partner(k)
            pltpu.make_async_remote_copy(
                src_ref=src.at[inner_index(px, pz, pc)],
                dst_ref=dst.at[mine],
                send_sem=send_sem,
                recv_sem=recv_sem.at[c, k // SPLIT],
                device_id={"latent": latent_index(px, pz, pc)},
                device_id_type=MESH,
            ).start()
            return 0

        lax.fori_loop(first, last, one, 0)
        if last == N - 1:
            pltpu.make_async_copy(src.at[mine], dst.at[mine], recv_sem.at[c, 0]).start()

    def take(ref, sem):
        pltpu.make_async_copy(ref, ref, sem).wait()

    with jax.named_scope("spread_tokens"):
        loads[0].wait()
        loads[1].start()
        loads[2].start()
        spread(tokens)
        pack(sx)
    with jax.named_scope("entry_wait"):
        pl.semaphore_wait(barrier, N - 1 + NY - 1)

    @pl.when(c == 0)
    def _():
        send_rows(sx, rx, sx_sem, rx_sem, 0, FIRST)

    masked = lax.rem(z, NY) == y

    @pl.when(masked)
    def _():
        ids = slots[...]
        member = [jnp.zeros((LANE, rows), F32) for _ in range(2)]
        for k in range(slots.shape[0]):
            one_id = ids[k : k + 1, :]
            member = [jnp.where(one_id == subs + b * LANE, 1.0, member[b]) for b in range(2)]
        member = [m.astype(BF16) for m in member]
        sub16 = lax.broadcasted_iota(jnp.int32, (SUB, rows), 0)
        for px in range(NX):
            for pc in range(NC):
                goes = [place[b : b + 1, :] == inner_index(px, sub16, pc) for b in range(2)]
                for r in range(CAP):
                    s1[px, (pc * CAP + r) * SUB : (pc * CAP + r + 1) * SUB, :] = sum(
                        lax.dot_general(
                            jnp.where(goes[b] & (rank[b] == r), 1.0, 0.0).astype(BF16),
                            member[b],
                            (((1,), (1,)), ((), ())),
                            preferred_element_type=F32,
                        )
                        for b in range(2)
                    ).astype(BF16)
        for k in range(NX):
            px = lax.rem(x + k, NX)
            copy = pltpu.make_async_remote_copy(
                src_ref=s1.at[px],
                dst_ref=r1.at[c * NX + x],
                send_sem=s1_sem,
                recv_sem=r1_sem,
                device_id={"latent": latent_index(px, z, 1)},
                device_id_type=MESH,
            )
            if k:
                copy.start()
            else:
                pl.when(c == 0)(copy.start)

        @pl.when(c == 1)
        def _():
            pltpu.make_async_copy(s1.at[x], r1.at[NX + x], r1_sem).start()

    @pl.when(c == 0)
    def _():
        send_rows(sx, rx, sx_sem, rx_sem, FIRST)

    @pl.when(masked & (c == 1))
    def _():
        take(r1, r1_sem)
        ro = lax.broadcasted_iota(jnp.int32, (NZ * 2 * SUB, NC * NX * CHUNK), 0)
        co = lax.broadcasted_iota(jnp.int32, (NZ * 2 * SUB, NC * NX * CHUNK), 1)
        from_x, from_r, from_c, to_z = ro & 3, (ro >> 2) & 3, (ro >> 4) & 1, ro >> 5
        origin = (from_c * NX + from_x) * CHUNK + from_r * NZ + to_z
        order = jnp.where((from_r < CAP) & (co == origin), 1.0, 0.0).astype(BF16)
        for pc in range(NC):
            got = r1[:, pc * CHUNK : (pc + 1) * CHUNK, :].reshape(NC * NX * CHUNK, LANE)
            out = jnp.dot(order, got, preferred_element_type=F32).astype(BF16)
            s2[pc] = out.reshape(NZ, 2 * SUB, LANE)

        def one(k, _):
            pz, pc = lax.rem(z + z_step(k // NC), NZ), lax.rem(c + lax.rem(k, NC), NC)
            pltpu.make_async_remote_copy(
                src_ref=s2.at[pc, pz],
                dst_ref=r2.at[z // NY],
                send_sem=s2_sem,
                recv_sem=r2_sem,
                device_id={"latent": latent_index(x, pz, pc)},
                device_id_type=MESH,
            ).start()
            return 0

        lax.fori_loop(1, NZ * NC, one, 0)
        pltpu.make_async_copy(s2.at[1, z], r2.at[z // NY], r2_sem).start()

    def unpack(src, dst, h):
        for g in range(h * (HALF // SUB * CAP), (h + 1) * (HALF // SUB * CAP)):
            to_rows(src, g // CAP * SUB, g % CAP, dst, g * SUB)

    def contract(left, right, h):
        lhs = left[pl.ds(h * NX * CHUNK, NX * CHUNK), :]
        out = lax.dot_general(lhs, right[...], (((1,), (1,)), ((), ())), preferred_element_type=F32)
        return out.reshape(NX, CHUNK, LANE)

    def scatter(part, total, h, q):
        for k in range(1, NY):
            p = lax.rem(y + k, NY)
            pltpu.make_async_remote_copy(
                src_ref=part.at[h, p],
                dst_ref=total.at[h, k],
                send_sem=sf_sem.at[q, h],
                recv_sem=rf_sem.at[q, h],
                device_id={"tok": p},
                device_id_type=MESH,
            ).start()

    def summed(part, total, h, q):
        take(total.at[h, pl.ds(1, NY - 1)], rf_sem.at[q, h])
        out = part[h, y]
        for k in range(1, NY):
            out = out + total[h, k]
        return out

    def gather(values, h, q):
        for k in range(1, NY):
            pltpu.make_async_remote_copy(
                src_ref=values.at[h, y],
                dst_ref=values.at[h, y],
                send_sem=sg_sem.at[q, h],
                recv_sem=rg_sem.at[q, h],
                device_id={"tok": lax.rem(y + k, NY)},
                device_id_type=MESH,
            ).start()

    def gathered(values, h, q):
        take(values.at[h, pl.ds(0, NY - 1)], rg_sem.at[q, h])

    def forward(h):
        if h == 0:
            loads[1].wait()
        unpack(rx, xnat, h)
        part_f[h] = contract(xnat, enc, h)
        scatter(part_f, sum_f, h, 0)
        if h == 0:
            take(r2, r2_sem)
            ri = lax.broadcasted_iota(jnp.int32, (CHUNK, NY * SUB), 0)
            ci = lax.broadcasted_iota(jnp.int32, (CHUNK, NY * SUB), 1)
            pick = jnp.where(
                ci == ((ri >> 2) & 3) * SUB + (ri >> 4) * NX + (ri & 3), 1.0, 0.0
            ).astype(BF16)
            for i in range(NC):
                got = r2[:, i * SUB : (i + 1) * SUB, :].reshape(NY * SUB, LANE)
                mask[i] = jnp.dot(pick, got, preferred_element_type=F32)
        total = summed(part_f, sum_f, h, 0)
        codes[h, y] = (mask[h] * (total + bias[...])).astype(BF16)
        gather(codes, h, 0)
        gathered(codes, h, 0)
        if h == 0:
            loads[2].wait()
        mine_codes = codes[h].reshape(NX * CHUNK, LANE)

        def product(i, _):
            cols = pl.ds(pl.multiple_of(i * step, step), step)
            nat[pl.ds(h * NX * CHUNK, NX * CHUNK), cols] = jnp.dot(
                mine_codes, dec[:, cols], preferred_element_type=F32
            ).astype(BF16)
            return 0

        lax.fori_loop(0, width // step, product, 0)

        for g in range(h * (HALF // SUB * CAP), (h + 1) * (HALF // SUB * CAP)):
            to_tiles(nat, g * SUB, sp, g // CAP * SUB, g % CAP)

        def send(k, _):
            px, pz = lax.rem(x + lax.rem(k, NX), NX), lax.rem(z + z_step(k // NX), NZ)
            pltpu.make_async_remote_copy(
                src_ref=sp.at[inner_index(px, pz, h)],
                dst_ref=rp.at[mine],
                send_sem=sp_sem.at[h],
                recv_sem=rp_sem,
                device_id={"latent": latent_index(px, pz, h)},
                device_id_type=MESH,
            ).start()
            return 0

        @pl.when(c == h)
        def _():
            pltpu.make_async_copy(sp.at[mine], rp.at[mine], rp_sem).start()

        @pl.when(c != h)
        def _():
            send(0, 0)

        lax.fori_loop(0, HALF - 1, lambda i, _: send(HALF - 1 - i, _), 0)

    with jax.named_scope("rows_first_part"):
        take(rx.at[pl.ds(0, HALF // 2)], rx_sem.at[0, 1])

    @pl.when(c == 1)
    def _():
        send_rows(sx, rx, sx_sem, rx_sem)

    with jax.named_scope("rows_of_core_0"):
        take(rx.at[pl.ds(0, HALF // 2)], rx_sem.at[0, 0])
    with jax.named_scope("forward_core_0"):
        forward(0)
    with jax.named_scope("rows_of_core_1"):
        take(rx.at[pl.ds(HALF, HALF // 2)], rx_sem.at[1, 1])
        take(rx.at[pl.ds(HALF, HALF // 2)], rx_sem.at[1, 0])
    with jax.named_scope("forward_core_1"):
        forward(1)

    with jax.named_scope("partials"):
        take(rp, rp_sem)

    for g in range(CAP * N // SUB):
        to_rows(rp, g % (N // SUB) * SUB, g // (N // SUB), nat, g * SUB)

    collect = smat[...].astype(F32).T.astype(BF16)

    def error(i, _):
        cols = pl.ds(pl.multiple_of(i * step, step), step)
        recon = jnp.dot(collect, nat[:, cols], preferred_element_type=F32)
        err = (recon - tokens[:, cols].astype(F32)).astype(BF16)
        nat[:, cols] = jnp.dot(
            smat[...], err, preferred_element_type=F32
        ).astype(BF16)
        return 0

    with jax.named_scope("error_rows"):
        lax.fori_loop(0, width // step, error, 0)
        pack(se)
    with jax.named_scope("send_errors"):
        send_rows(se, re, se_sem, re_sem)

    scale = math.sqrt(LANE / (rows * slots.shape[0]))
    half_rows = NX * CHUNK

    def turned(values, h):
        return values[h].reshape(half_rows, LANE).astype(F32).T.astype(BF16)

    def arrived(h):
        with jax.named_scope("errors_of_core_%d" % h):
            take(re.at[pl.ds(h * HALF, HALF // 2)], re_sem.at[h, 1])
            take(re.at[pl.ds(h * HALF, HALF // 2)], re_sem.at[h, 0])
        unpack(re, enat, h)
        part_b[h] = contract(enat, dec, h)
        scatter(part_b, sum_b, h, 1)

    def finish(h):
        back[h, y] = (mask[h] * summed(part_b, sum_b, h, 1)).astype(BF16)
        gather(back, h, 1)

    def half_product(left, other, h, cols):
        return jnp.dot(
            left, other[h * half_rows : (h + 1) * half_rows, cols], preferred_element_type=F32
        )

    pieces = [slice(i * step, (i + 1) * step) for i in range(width // step)]
    code_rows = [turned(codes, h) for h in range(NC)]
    arrived(0)
    finish(0)
    arrived(1)
    for cols in pieces:
        gdec[:, cols] = (
            sum(half_product(code_rows[h], enat, h, cols) for h in range(NC)) * scale
        ).astype(BF16)
    finish(1)
    gathered(back, 0, 1)
    left = turned(back, 0)
    for cols in pieces:
        early[:, cols] = half_product(left, xnat, 0, cols)
    gathered(back, 1, 1)
    left = turned(back, 1)
    for cols in pieces:
        genc[:, cols] = ((early[:, cols] + half_product(left, xnat, 1, cols)) * scale).astype(BF16)

    take(sx.at[pl.ds(0, N - 1)], sx_sem)
    take(se.at[pl.ds(0, N - 1)], se_sem)

    @pl.when(masked)
    def _():
        take(s1.at[pl.ds(0, NX - 1)], s1_sem)

        @pl.when(c == 0)
        def _():
            take(s1.at[0], s1_sem)

        @pl.when(c == 1)
        def _():
            take(s2.at[0], s2_sem)
            take(s2.at[1, pl.ds(0, NZ - 1)], s2_sem)

    for h in range(NC):

        @pl.when(c == h)
        def _(h=h):
            take(sp.at[pl.ds(0, HALF - 1)], sp_sem.at[h])

        @pl.when(c != h)
        def _(h=h):
            take(sp.at[pl.ds(0, HALF)], sp_sem.at[h])

        take(part_f.at[h, pl.ds(0, NY - 1)], sf_sem.at[0, h])
        take(part_b.at[h, pl.ds(0, NY - 1)], sf_sem.at[1, h])
        take(codes.at[h, pl.ds(0, NY - 1)], sg_sem.at[0, h])
        take(back.at[h, pl.ds(0, NY - 1)], sg_sem.at[1, h])


def local(tokens, blocks, slots, enc, dec, bias):
    rows, width = tokens.shape
    tiles = pltpu.VMEM((N, CAP, SUB, LANE), BF16)
    dense = pltpu.VMEM((CAP * N, width), BF16)
    shares = pltpu.VMEM((NC, NY, CHUNK, LANE), F32)
    shares16 = pltpu.VMEM((NC, NY, CHUNK, LANE), BF16)
    dma = pltpu.SemaphoreType.DMA
    hbm, vmem = pltpu.HBM, pltpu.VMEM
    return pl.pallas_call(
        kernel,
        out_shape=[jax.ShapeDtypeStruct((rows, width), BF16)] * 2,
        in_specs=[pl.BlockSpec(memory_space=m) for m in (hbm, vmem, vmem, hbm, hbm, vmem)],
        out_specs=[pl.BlockSpec(memory_space=vmem)] * 2,
        scratch_shapes=[pltpu.VMEM((rows, width), BF16)] * 3
        + [tiles] * 6
        + [
            pltpu.VMEM((NX, NC * CHUNK, LANE), BF16),
            pltpu.VMEM((NC * NX, NC * CHUNK, LANE), BF16),
            pltpu.VMEM((NC, NZ, 2 * SUB, LANE), BF16),
            pltpu.VMEM((NY, 2 * SUB, LANE), BF16),
            dense,
            dense,
            dense,
            pltpu.VMEM((CAP * N, rows), BF16),
            pltpu.VMEM((rows, width), F32),
            shares,
            shares,
            shares,
            shares,
            shares16,
            shares16,
            pltpu.VMEM((NC, CHUNK, LANE), F32),
            dma,
            dma((NC,)),
            dma,
            dma,
            dma,
            dma((NC, 2)),
            dma,
            dma((NC, 2)),
            dma,
            dma,
            dma((2, NC)),
            dma((2, NC)),
            dma((2, NC)),
            dma((2, NC)),
            dma((3,)),
        ],
        compiler_params=pltpu.CompilerParams(
            collective_id=0, has_side_effects=True, vmem_limit_bytes=60 << 20
        ),
    )(tokens, blocks.T, slots.T, enc, dec, bias.reshape(1, -1))


def solution(mesh):
    placed = (
        P("latent", "tok"),
        P("latent", None),
        P("latent", None),
        P("latent", "tok"),
        P("latent", "tok"),
        P("latent"),
    )
    return jax.shard_map(
        local,
        mesh=mesh,
        in_specs=placed,
        out_specs=(P("latent", "tok"), P("latent", "tok")),
        check_vma=False,
    )
```

time: 273 us -> 246 us (0.901)
  Pallas kernels: 264 us -> 239 us
  local copies, waits for them, and re-layouts: 6.79 us -> 2.74 us
    pallas_call x1, Pallas kernels: 264 us -> 239 us  [local(): pl.pallas_call(kernel, out_shape=[jax.ShapeDtypeStruct((rows, width), BF1...]
    unnamed x16 -> x4, local copies, waits for them, and re-layouts: 6.79 us -> 2.74 us
where the time goes in v2:
time: 246 us; the launch traced here: 242 us
  Pallas kernels  239 us (97%)
  local copies, waits for them, and re-layouts  2.74 us (1%)
    pallas_call x1, Pallas kernels, local(): pl.pallas_call(kernel, out_shape=[jax.ShapeDtypeStruct((rows, width), BF1...  239 us

profile of v2, /device:TPU:1, one launch (start us, length us, event | category | flops | bytes accessed | tf_op | source)
XLA Modules:
  0.0 242.4 jit_solution(10263910433297531770)
XLA Ops:
  0.6 239.0 %shard_map.77 = (bf16[128,2048]{1,0:T(8,128)(2,1)}, bf16[128,2048]{1,0:T(8,128)(2,1)}) custom-call(bf16[128,2048]{1,0:T(8,128)(2,1)} %tokens_hbm.1, s32[2,128]{1,0:T(2,128)} %bitcast.4, s32[64,128]{1,0:T(8,128)} %bitcast.3, bf16[128,2048]{1,0:T(8,128)(2,1)} %enc_hbm.1, bf16[128,2048]{1,0:T(8,128)(2,1)} %dec_hbm.1, f32[1,128]{1,0:T(1,128)} %bitcast.5), custom_call_target="tpu_custom_call" | custom-call | tf_op jit(solution)/shard_map/pallas_call | solution.py:459
  239.6 0.0 copy-start
  239.7 1.9 copy.10
  241.6 0.0 copy-done
  241.6 0.8 copy.11
Async XLA Ops:
  239.6 2.0 copy-start

commit v3 on v2

--- a/solution.py
+++ b/solution.py
@@ -20,8 +20,9 @@
 SUB = 16
 LANE = 128
 CHUNK = CAP * NZ
-SPLIT = N // 2
-FIRST = 32
+SPLIT = 32
+FIRST = 16
+OTHERS = N - NZ
 
 
 def latent_index(x, z, c):
@@ -37,14 +38,14 @@
 
 
 def kernel(
-    tokens_hbm, blocks, slots, enc_hbm, dec_hbm, bias,
+    tokens_hbm, blocks_hbm, slots_hbm, enc_hbm, dec_hbm, bias_hbm,
     genc, gdec,
-    tokens, enc, dec,
+    tokens, blocks, slots, enc, dec, bias,
     sx, rx, sp, rp, se, re, s1, r1, s2, r2,
     nat, xnat, enat, smat, early,
-    part_f, part_b, sum_f, sum_b, codes, back, mask,
+    part_f, part_b, sum_f, sent_b, sum_b, codes, back, mask, mask_all,
     sx_sem, sp_sem, se_sem, s1_sem, s2_sem, rx_sem, rp_sem, re_sem, r1_sem, r2_sem,
-    sf_sem, rf_sem, sg_sem, rg_sem, in_sem,
+    sf_sem, rf_sem, sg_sem, rg_sem, in_sem, line_sem,
 ):
     width = tokens.shape[1]
     rows = tokens.shape[0]
@@ -64,19 +65,30 @@
 
     loads = [
         pltpu.make_async_copy(src, dst, in_sem.at[i])
-        for i, (src, dst) in enumerate(((tokens_hbm, tokens), (enc_hbm, enc), (dec_hbm, dec)))
+        for i, (src, dst) in enumerate(
+            (
+                (tokens_hbm, tokens),
+                (enc_hbm, enc),
+                (dec_hbm, dec),
+                (blocks_hbm, blocks),
+                (slots_hbm, slots),
+                (bias_hbm, bias),
+            )
+        )
     ]
+    loads[3].start()
     loads[0].start()
+    loads[4].start()
+    loads[5].start()
 
     barrier = pltpu.get_barrier_semaphore()
-
-    def greet(k, _):
-        pl.semaphore_signal(
-            barrier, inc=1, device_id={"latent": latent_index(*partner(k))}, device_id_type=MESH
-        )
-        return 0
-
-    lax.fori_loop(1, N, greet, 0)
+    line_ids = [latent_index(x, lax.rem(z + k, NZ), c) for k in range(1, NZ)]
+    plane_ids = [
+        latent_index(lax.rem(x + k // NC, NX), z, lax.rem(c + k % NC, NC))
+        for k in range(1, NX * NC)
+    ]
+    for peer in line_ids + plane_ids:
+        pl.semaphore_signal(barrier, inc=1, device_id={"latent": peer}, device_id_type=MESH)
     for k in range(1, NY):
         pl.semaphore_signal(
             barrier, inc=1, device_id={"tok": lax.rem(y + k, NY)}, device_id_type=MESH
@@ -94,6 +106,7 @@
 
     lanes = lax.broadcasted_iota(jnp.int32, (N, rows), 1)
     subs = lax.broadcasted_iota(jnp.int32, (N, rows), 0)
+    loads[3].wait()
     named = blocks[...]
     column = named // NC
     place = inner_index(column // NZ, lax.rem(column, NZ), lax.rem(named, NC))
@@ -125,22 +138,25 @@
         for g in range(CAP * N // SUB):
             to_tiles(nat, g * SUB, dst, g % (N // SUB) * SUB, g // (N // SUB))
 
-    def send_rows(src, dst, send_sem, recv_sem, first=0, last=N - 1):
-        def one(i, _):
-            k = N - 1 - i
+    def send_rows(src, dst, send_sem, recv_sem, first, last):
+        def one(k):
             px, pz, pc = partner(k)
             pltpu.make_async_remote_copy(
                 src_ref=src.at[inner_index(px, pz, pc)],
                 dst_ref=dst.at[mine],
                 send_sem=send_sem,
-                recv_sem=recv_sem.at[c, k // SPLIT],
+                recv_sem=recv_sem.at[c, (k + N - SPLIT) // N],
                 device_id={"latent": latent_index(px, pz, pc)},
                 device_id_type=MESH,
             ).start()
             return 0
 
-        lax.fori_loop(first, last, one, 0)
-        if last == N - 1:
+        group = NX * NC
+        if first == 0:
+            lax.fori_loop(0, NZ - 1, lambda i, _: one((NZ - 1 - i) * group), 0)
+        others = lambda i, _: one((NZ - 1 - i // (group - 1)) * group + 1 + lax.rem(i, group - 1))
+        lax.fori_loop(first or 0, last, others, 0)
+        if last == OTHERS:
             pltpu.make_async_copy(src.at[mine], dst.at[mine], recv_sem.at[c, 0]).start()
 
     def take(ref, sem):
@@ -148,16 +164,26 @@
 
     with jax.named_scope("spread_tokens"):
         loads[0].wait()
+        loads[4].wait()
+        loads[5].wait()
         loads[1].start()
         loads[2].start()
         spread(tokens)
         pack(sx)
     with jax.named_scope("entry_wait"):
-        pl.semaphore_wait(barrier, N - 1 + NY - 1)
+        pl.semaphore_wait(barrier, NZ - 1 + NX * NC - 1 + NY - 1)
+    for peer in plane_ids:
+        pl.semaphore_signal(line_sem, inc=1, device_id={"latent": peer}, device_id_type=MESH)
 
     @pl.when(c == 0)
     def _():
-        send_rows(sx, rx, sx_sem, rx_sem, 0, FIRST)
+        send_rows(sx, rx, sx_sem, rx_sem, 0, 0)
+
+    pl.semaphore_wait(line_sem, NX * NC - 1)
+
+    @pl.when(c == 0)
+    def _():
+        send_rows(sx, rx, sx_sem, rx_sem, None, FIRST)
 
     masked = lax.rem(z, NY) == y
 
@@ -204,7 +230,7 @@
 
     @pl.when(c == 0)
     def _():
-        send_rows(sx, rx, sx_sem, rx_sem, FIRST)
+        send_rows(sx, rx, sx_sem, rx_sem, FIRST, OTHERS)
 
     @pl.when(masked & (c == 1))
     def _():
@@ -292,6 +318,8 @@
             for i in range(NC):
                 got = r2[:, i * SUB : (i + 1) * SUB, :].reshape(NY * SUB, LANE)
                 mask[i] = jnp.dot(pick, got, preferred_element_type=F32)
+                mask_all[i, y] = mask[i].astype(BF16)
+                gather(mask_all, i, 1)
         total = summed(part_f, sum_f, h, 0)
         codes[h, y] = (mask[h] * (total + bias[...])).astype(BF16)
         gather(codes, h, 0)
@@ -335,19 +363,19 @@
         lax.fori_loop(0, HALF - 1, lambda i, _: send(HALF - 1 - i, _), 0)
 
     with jax.named_scope("rows_first_part"):
-        take(rx.at[pl.ds(0, HALF // 2)], rx_sem.at[0, 1])
+        take(rx.at[pl.ds(0, 48)], rx_sem.at[0, 1])
 
     @pl.when(c == 1)
     def _():
-        send_rows(sx, rx, sx_sem, rx_sem)
+        send_rows(sx, rx, sx_sem, rx_sem, 0, OTHERS)
 
     with jax.named_scope("rows_of_core_0"):
-        take(rx.at[pl.ds(0, HALF // 2)], rx_sem.at[0, 0])
+        take(rx.at[pl.ds(0, 16)], rx_sem.at[0, 0])
     with jax.named_scope("forward_core_0"):
         forward(0)
     with jax.named_scope("rows_of_core_1"):
-        take(rx.at[pl.ds(HALF, HALF // 2)], rx_sem.at[1, 1])
-        take(rx.at[pl.ds(HALF, HALF // 2)], rx_sem.at[1, 0])
+        take(rx.at[pl.ds(HALF, 48)], rx_sem.at[1, 1])
+        take(rx.at[pl.ds(HALF, 16)], rx_sem.at[1, 0])
     with jax.named_scope("forward_core_1"):
         forward(1)
 
@@ -372,7 +400,7 @@
         lax.fori_loop(0, width // step, error, 0)
         pack(se)
     with jax.named_scope("send_errors"):
-        send_rows(se, re, se_sem, re_sem)
+        send_rows(se, re, se_sem, re_sem, 0, OTHERS)
 
     scale = math.sqrt(LANE / (rows * slots.shape[0]))
     half_rows = NX * CHUNK
@@ -382,15 +410,27 @@
 
     def arrived(h):
         with jax.named_scope("errors_of_core_%d" % h):
-            take(re.at[pl.ds(h * HALF, HALF // 2)], re_sem.at[h, 1])
-            take(re.at[pl.ds(h * HALF, HALF // 2)], re_sem.at[h, 0])
+            take(re.at[pl.ds(h * HALF, 48)], re_sem.at[h, 1])
+            take(re.at[pl.ds(h * HALF, 16)], re_sem.at[h, 0])
         unpack(re, enat, h)
         part_b[h] = contract(enat, dec, h)
-        scatter(part_b, sum_b, h, 1)
+        sent_b[h] = part_b[h].astype(BF16)
+        for k in range(1, NY):
+            pltpu.make_async_remote_copy(
+                src_ref=sent_b.at[h],
+                dst_ref=sum_b.at[h, k],
+                send_sem=sf_sem.at[1, h],
+                recv_sem=rf_sem.at[1, h],
+                device_id={"tok": lax.rem(y + k, NY)},
+                device_id_type=MESH,
+            ).start()
 
     def finish(h):
-        back[h, y] = (mask[h] * summed(part_b, sum_b, h, 1)).astype(BF16)
-        gather(back, h, 1)
+        take(sum_b.at[h, pl.ds(1, NY - 1)], rf_sem.at[1, h])
+        total = part_b[h]
+        for k in range(1, NY):
+            total = total + sum_b[h, k].astype(F32)
+        back[h] = (mask_all[h].astype(F32) * total).astype(BF16)
 
     def half_product(left, other, h, cols):
         return jnp.dot(
@@ -400,18 +440,18 @@
     pieces = [slice(i * step, (i + 1) * step) for i in range(width // step)]
     code_rows = [turned(codes, h) for h in range(NC)]
     arrived(0)
+    arrived(1)
+    for h in range(NC):
+        gathered(mask_all, h, 1)
     finish(0)
-    arrived(1)
     for cols in pieces:
         gdec[:, cols] = (
             sum(half_product(code_rows[h], enat, h, cols) for h in range(NC)) * scale
         ).astype(BF16)
-    finish(1)
-    gathered(back, 0, 1)
     left = turned(back, 0)
     for cols in pieces:
         early[:, cols] = half_product(left, xnat, 0, cols)
-    gathered(back, 1, 1)
+    finish(1)
     left = turned(back, 1)
     for cols in pieces:
         genc[:, cols] = ((early[:, cols] + half_product(left, xnat, 1, cols)) * scale).astype(BF16)
@@ -443,9 +483,9 @@
             take(sp.at[pl.ds(0, HALF)], sp_sem.at[h])
 
         take(part_f.at[h, pl.ds(0, NY - 1)], sf_sem.at[0, h])
-        take(part_b.at[h, pl.ds(0, NY - 1)], sf_sem.at[1, h])
+        take(sum_b.at[h, pl.ds(1, NY - 1)], sf_sem.at[1, h])
         take(codes.at[h, pl.ds(0, NY - 1)], sg_sem.at[0, h])
-        take(back.at[h, pl.ds(0, NY - 1)], sg_sem.at[1, h])
+        take(mask_all.at[h, pl.ds(0, NY - 1)], sg_sem.at[1, h])
 
 
 def local(tokens, blocks, slots, enc, dec, bias):
@@ -456,12 +496,13 @@
     shares16 = pltpu.VMEM((NC, NY, CHUNK, LANE), BF16)
     dma = pltpu.SemaphoreType.DMA
     hbm, vmem = pltpu.HBM, pltpu.VMEM
+    args = (tokens, blocks.T, slots.T, enc, dec, bias.reshape(1, -1))
     return pl.pallas_call(
         kernel,
         out_shape=[jax.ShapeDtypeStruct((rows, width), BF16)] * 2,
-        in_specs=[pl.BlockSpec(memory_space=m) for m in (hbm, vmem, vmem, hbm, hbm, vmem)],
+        in_specs=[pl.BlockSpec(memory_space=hbm)] * 6,
         out_specs=[pl.BlockSpec(memory_space=vmem)] * 2,
-        scratch_shapes=[pltpu.VMEM((rows, width), BF16)] * 3
+        scratch_shapes=[pltpu.VMEM(a.shape, a.dtype) for a in args]
         + [tiles] * 6
         + [
             pltpu.VMEM((NX, NC * CHUNK, LANE), BF16),
@@ -476,10 +517,12 @@
             shares,
             shares,
             shares,
-            shares,
+            shares16,
+            pltpu.VMEM((NC, NY, NY, CHUNK, LANE), BF16),
             shares16,
             shares16,
             pltpu.VMEM((NC, CHUNK, LANE), F32),
+            shares16,
             dma,
             dma((NC,)),
             dma,
@@ -494,12 +537,13 @@
             dma((2, NC)),
             dma((2, NC)),
             dma((2, NC)),
-            dma((3,)),
+            dma((6,)),
+            pltpu.SemaphoreType.REGULAR,
         ],
         compiler_params=pltpu.CompilerParams(
-            collective_id=0, has_side_effects=True, vmem_limit_bytes=60 << 20
+            collective_id=0, has_side_effects=True, vmem_limit_bytes=36 << 20
         ),
-    )(tokens, blocks.T, slots.T, enc, dec, bias.reshape(1, -1))
+    )(*[pltpu.with_memory_space_constraint(a, hbm) for a in args])
 
 
 def solution(mesh):

time: 246 us -> 235 us (0.955); the launches traced: 242 us -> 235 us
  Pallas kernels: 239 us -> 233 us
    pallas_call x1, Pallas kernels: 239 us -> 233 us  [local(): pl.pallas_call(kernel, out_shape=[jax.ShapeDtypeStruct((rows, width), BF1...]
where the time goes in v3:
time: 235 us
  Pallas kernels  233 us (99%)
    pallas_call x1, Pallas kernels, local(): pl.pallas_call(kernel, out_shape=[jax.ShapeDtypeStruct((rows, width), BF1...  233 us

profile of v3, /device:TPU:1, one launch (start us, length us, event | category | flops | bytes accessed | tf_op | source)
XLA Modules:
  0.0 234.9 jit_solution(12374184316979416760)
XLA Ops:
  0.6 232.7 %shard_map.77 = (bf16[128,2048]{1,0:T(8,128)(2,1)S(1)}, bf16[128,2048]{1,0:T(8,128)(2,1)S(1)}) custom-call(bf16[128,2048]{1,0:T(8,128)(2,1)} %tokens_hbm.1, s32[2,128]{1,0:T(2,128)} %bitcast.4, s32[64,128]{1,0:T(8,128)} %bitcast.3, bf16[128,2048]{1,0:T(8,128)(2,1)} %enc_hbm.1, bf16[128,2048]{1,0:T(8,128)(2,1)} %dec_hbm.1, f32[1,128]{1,0:T(1,128)} %bitcast.5), custom_call_target="tpu_custom_call" | custom-call | tf_op jit(solution)/shard_map/pallas_call | solution.py:500
  233.3 0.8 copy.10
  234.1 0.8 copy.11

commit v4 on v3

--- a/solution.py
+++ b/solution.py
@@ -20,7 +20,7 @@
 SUB = 16
 LANE = 128
 CHUNK = CAP * NZ
-SPLIT = 32
+SPLIT = 48
 FIRST = 16
 OTHERS = N - NZ
 
@@ -125,14 +125,11 @@
         ).astype(BF16)
 
     step = 512
+    pieces = [slice(i * step, (i + 1) * step) for i in range(width // step)]
 
     def spread(src):
-        def one(i, _):
-            cols = pl.ds(pl.multiple_of(i * step, step), step)
+        for cols in pieces:
             nat[:, cols] = jnp.dot(smat[...], src[:, cols], preferred_element_type=F32).astype(BF16)
-            return 0
-
-        lax.fori_loop(0, width // step, one, 0)
 
     def pack(dst):
         for g in range(CAP * N // SUB):
@@ -328,14 +325,10 @@
             loads[2].wait()
         mine_codes = codes[h].reshape(NX * CHUNK, LANE)
 
-        def product(i, _):
-            cols = pl.ds(pl.multiple_of(i * step, step), step)
-            nat[pl.ds(h * NX * CHUNK, NX * CHUNK), cols] = jnp.dot(
+        for cols in pieces:
+            nat[h * NX * CHUNK : (h + 1) * NX * CHUNK, cols] = jnp.dot(
                 mine_codes, dec[:, cols], preferred_element_type=F32
             ).astype(BF16)
-            return 0
-
-        lax.fori_loop(0, width // step, product, 0)
 
         for g in range(h * (HALF // SUB * CAP), (h + 1) * (HALF // SUB * CAP)):
             to_tiles(nat, g * SUB, sp, g // CAP * SUB, g % CAP)
@@ -363,19 +356,19 @@
         lax.fori_loop(0, HALF - 1, lambda i, _: send(HALF - 1 - i, _), 0)
 
     with jax.named_scope("rows_first_part"):
-        take(rx.at[pl.ds(0, 48)], rx_sem.at[0, 1])
+        take(rx.at[pl.ds(0, 40)], rx_sem.at[0, 1])
 
     @pl.when(c == 1)
     def _():
         send_rows(sx, rx, sx_sem, rx_sem, 0, OTHERS)
 
     with jax.named_scope("rows_of_core_0"):
-        take(rx.at[pl.ds(0, 16)], rx_sem.at[0, 0])
+        take(rx.at[pl.ds(0, 24)], rx_sem.at[0, 0])
     with jax.named_scope("forward_core_0"):
         forward(0)
     with jax.named_scope("rows_of_core_1"):
-        take(rx.at[pl.ds(HALF, 48)], rx_sem.at[1, 1])
-        take(rx.at[pl.ds(HALF, 16)], rx_sem.at[1, 0])
+        take(rx.at[pl.ds(HALF, 40)], rx_sem.at[1, 1])
+        take(rx.at[pl.ds(HALF, 24)], rx_sem.at[1, 0])
     with jax.named_scope("forward_core_1"):
         forward(1)
 
@@ -387,22 +380,20 @@
 
     collect = smat[...].astype(F32).T.astype(BF16)
 
-    def error(i, _):
-        cols = pl.ds(pl.multiple_of(i * step, step), step)
+    def error(cols):
         recon = jnp.dot(collect, nat[:, cols], preferred_element_type=F32)
         err = (recon - tokens[:, cols].astype(F32)).astype(BF16)
         nat[:, cols] = jnp.dot(
             smat[...], err, preferred_element_type=F32
         ).astype(BF16)
-        return 0
 
     with jax.named_scope("error_rows"):
-        lax.fori_loop(0, width // step, error, 0)
+        for cols in pieces:
+            error(cols)
         pack(se)
     with jax.named_scope("send_errors"):
         send_rows(se, re, se_sem, re_sem, 0, OTHERS)
 
-    scale = math.sqrt(LANE / (rows * slots.shape[0]))
     half_rows = NX * CHUNK
 
     def turned(values, h):
@@ -410,8 +401,8 @@
 
     def arrived(h):
         with jax.named_scope("errors_of_core_%d" % h):
-            take(re.at[pl.ds(h * HALF, 48)], re_sem.at[h, 1])
-            take(re.at[pl.ds(h * HALF, 16)], re_sem.at[h, 0])
+            take(re.at[pl.ds(h * HALF, 40)], re_sem.at[h, 1])
+            take(re.at[pl.ds(h * HALF, 24)], re_sem.at[h, 0])
         unpack(re, enat, h)
         part_b[h] = contract(enat, dec, h)
         sent_b[h] = part_b[h].astype(BF16)
@@ -437,7 +428,6 @@
             left, other[h * half_rows : (h + 1) * half_rows, cols], preferred_element_type=F32
         )
 
-    pieces = [slice(i * step, (i + 1) * step) for i in range(width // step)]
     code_rows = [turned(codes, h) for h in range(NC)]
     arrived(0)
     arrived(1)
@@ -446,7 +436,7 @@
     finish(0)
     for cols in pieces:
         gdec[:, cols] = (
-            sum(half_product(code_rows[h], enat, h, cols) for h in range(NC)) * scale
+            sum(half_product(code_rows[h], enat, h, cols) for h in range(NC))
         ).astype(BF16)
     left = turned(back, 0)
     for cols in pieces:
@@ -454,7 +444,7 @@
     finish(1)
     left = turned(back, 1)
     for cols in pieces:
-        genc[:, cols] = ((early[:, cols] + half_product(left, xnat, 1, cols)) * scale).astype(BF16)
+        genc[:, cols] = (early[:, cols] + half_product(left, xnat, 1, cols)).astype(BF16)
 
     take(sx.at[pl.ds(0, N - 1)], sx_sem)
     take(se.at[pl.ds(0, N - 1)], se_sem)
@@ -497,7 +487,7 @@
     dma = pltpu.SemaphoreType.DMA
     hbm, vmem = pltpu.HBM, pltpu.VMEM
     args = (tokens, blocks.T, slots.T, enc, dec, bias.reshape(1, -1))
-    return pl.pallas_call(
+    genc, gdec = pl.pallas_call(
         kernel,
         out_shape=[jax.ShapeDtypeStruct((rows, width), BF16)] * 2,
         in_specs=[pl.BlockSpec(memory_space=hbm)] * 6,
@@ -544,6 +534,8 @@
             collective_id=0, has_side_effects=True, vmem_limit_bytes=36 << 20
         ),
     )(*[pltpu.with_memory_space_constraint(a, hbm) for a in args])
+    scale = jnp.asarray(math.sqrt(LANE / (rows * slots.shape[1])), BF16)
+    return genc * scale, gdec * scale
 
 
 def solution(mesh):

time: 235 us -> 233 us (level)
  no operation moved by 1% of the time
where the time goes in v4:
time: 233 us
  Pallas kernels  231 us (99%)
    pallas_call x1, Pallas kernels, local(): pl.pallas_call(kernel, out_shape=[jax.ShapeDtypeStruct((rows, width), BF1...  231 us

profile of v4, /device:TPU:1, one launch (start us, length us, event | category | flops | bytes accessed | tf_op | source)
XLA Modules:
  0.0 232.6 jit_solution(18191977566800666743)
XLA Ops:
  0.6 230.9 %shard_map.77 = (bf16[128,2048]{1,0:T(8,128)(2,1)S(1)}, bf16[128,2048]{1,0:T(8,128)(2,1)S(1)}) custom-call(bf16[128,2048]{1,0:T(8,128)(2,1)} %tokens_hbm.1, s32[2,128]{1,0:T(2,128)} %bitcast.4, s32[64,128]{1,0:T(8,128)} %bitcast.3, bf16[128,2048]{1,0:T(8,128)(2,1)} %enc_hbm.1, bf16[128,2048]{1,0:T(8,128)(2,1)} %dec_hbm.1, f32[1,128]{1,0:T(1,128)} %bitcast.5), custom_call_target="tpu_custom_call" | custom-call | tf_op jit(solution)/shard_map/pallas_call | solution.py:490
  231.5 1.1 broadcast_multiply_fusion

commit v5 on v4

--- a/solution.py
+++ b/solution.py
@@ -173,6 +173,10 @@
         pl.semaphore_signal(line_sem, inc=1, device_id={"latent": peer}, device_id_type=MESH)
 
     @pl.when(c == 0)
+    def _():
+        send_rows(sx, rx, sx_sem, rx_sem, 0, 0)
+
+    @pl.when(c == 1)
     def _():
         send_rows(sx, rx, sx_sem, rx_sem, 0, 0)
 
@@ -360,7 +364,7 @@
 
     @pl.when(c == 1)
     def _():
-        send_rows(sx, rx, sx_sem, rx_sem, 0, OTHERS)
+        send_rows(sx, rx, sx_sem, rx_sem, None, OTHERS)
 
     with jax.named_scope("rows_of_core_0"):
         take(rx.at[pl.ds(0, 24)], rx_sem.at[0, 0])

time: 233 us -> 231 us (level)
  no operation moved by 1% of the time
where the time goes in v5:
time: 231 us
  Pallas kernels  230 us (100%)
    pallas_call x1, Pallas kernels, local(): pl.pallas_call(kernel, out_shape=[jax.ShapeDtypeStruct((rows, width), BF1...  230 us

profile of v5, /device:TPU:1, one launch (start us, length us, event | category | flops | bytes accessed | tf_op | source)
XLA Modules:
  0.0 231.2 jit_solution(17457801541358961720)
XLA Ops:
  0.6 229.5 %shard_map.77 = (bf16[128,2048]{1,0:T(8,128)(2,1)S(1)}, bf16[128,2048]{1,0:T(8,128)(2,1)S(1)}) custom-call(bf16[128,2048]{1,0:T(8,128)(2,1)} %tokens_hbm.1, s32[2,128]{1,0:T(2,128)} %bitcast.4, s32[64,128]{1,0:T(8,128)} %bitcast.3, bf16[128,2048]{1,0:T(8,128)(2,1)} %enc_hbm.1, bf16[128,2048]{1,0:T(8,128)(2,1)} %dec_hbm.1, f32[1,128]{1,0:T(1,128)} %bitcast.5), custom_call_target="tpu_custom_call" | custom-call | tf_op jit(solution)/shard_map/pallas_call | solution.py:494
  230.1 1.1 broadcast_multiply_fusion
